TPU v7x, 128 devices: a whole 4x4x4 slice. The times are simulated.
128 devices in a mesh: dp: 4 (over z_hi, core), section: 8 (over z_lo, x), tensor: 4 (over y).
Axes of the slice: x: 4, y: 4, z: 4 (z_hi: 2, z_lo: 2; z = z_hi * 2 + z_lo), core: 2. Of those that a mesh axis runs over, the one named last changes fastest.
Arguments:
- queries: bfloat16 [8, 8192, 4096], P('section', 'dp', 'tensor'), may hold values from -68 to 68
- cotangent: bfloat16 [8, 8192, 4096], P('section', 'dp', 'tensor'), may hold values from -6 to 6
- vision: bfloat16 [2048, 8192], P(('dp', 'section', 'tensor')), may hold values from -6 to 6
- kv_weight: bfloat16 [8, 8192, 4, 256], P('section', 'dp', 'tensor'), may hold values from -0.0625 to 0.0625
- visible_tiles: int32 [4, 16, 8], P('dp'), may hold values from 0 to 1, as said below
- image_count: int32 [4], P('dp'), may hold values from 1 to 2
Outputs:
- context: bfloat16 [8, 8192, 4096], P('section', 'dp', 'tensor')
- grad_queries: bfloat16 [8, 8192, 4096], P('section', 'dp', 'tensor')
- grad_vision: float32 [2048, 8192], P(('dp', 'section', 'tensor'))
- grad_kv_weight: float32 [8, 8192, 4, 256], P('section', 'dp', 'tensor')
Inputs may be any that keep to these rules, and one draw needn't show every extreme that they name: `visible_tiles`: in every document one whole block of 128 text tokens sees no tile.
All inputs are finite; a program needn't handle non-finite values.
Results may differ from a plain program's by a relative error of at most 0.017.
The roundings to bfloat16 on the way count: a program that leaves them out, or rounds other values in their place, can miss the bound.
Values may be sent and summed in bfloat16 or wider, within the bound.
No kernel may reach another device: no remote copies, remote signals or barrier semaphores. Data moves between devices by JAX's collectives and lax.ppermute only.
A program may use at most 192 MiB of HBM per device.

v0:
```python
import jax
import jax.numpy as jnp
from jax import lax
from jax.sharding import PartitionSpec as P

HEADS = 32
KV = 4
HD = 128
TILES = 4
TEXT_BLOCK = 128
TILE_ROWS = 64
ROW_BLOCK = 512


def build_visible(tile_mask, image_total):
    key_tile = jnp.repeat(tile_mask, TILE_ROWS, axis=1)
    row_tile = jnp.repeat(key_tile, TEXT_BLOCK, axis=0)
    key_image = jnp.arange(row_tile.shape[1], dtype=jnp.int32) // (TILES * TILE_ROWS)
    return (row_tile == 1) & (key_image < image_total)[None, :]


def attend_block(query_part, cot_part, key_rows, value_rows, visible):
    score_scale = HD ** (-0.5)
    wide = jnp.float32
    scores = (
        jnp.einsum("rkgd,jkd->rkgj", query_part, key_rows, preferred_element_type=wide)
        * score_scale
    )
    seen = visible[:, None, None, :]
    any_seen = jnp.any(visible, axis=-1)[:, None, None, None]
    peak = jnp.max(jnp.where(seen, scores, -jnp.inf), axis=-1, keepdims=True)
    peak = jnp.where(any_seen, peak, jnp.zeros_like(peak))
    expon = jnp.where(seen, jnp.exp(scores - peak), jnp.zeros_like(scores))
    total = jnp.sum(expon, axis=-1, keepdims=True)
    total = jnp.where(any_seen, total, jnp.ones_like(total))
    probs = expon / total
    probs_low = probs.astype(jnp.bfloat16)
    context = jnp.einsum(
        "rkgj,jkd->rkgd", probs_low, value_rows, preferred_element_type=wide
    ).astype(jnp.bfloat16)
    prob_grad = jnp.einsum("rkgd,jkd->rkgj", cot_part, value_rows, preferred_element_type=wide)
    delta = jnp.sum(probs * prob_grad, axis=-1, keepdims=True)
    score_grad = (probs * (prob_grad - delta) * score_scale).astype(jnp.bfloat16)
    query_grad = jnp.einsum(
        "rkgj,jkd->rkgd", score_grad, key_rows, preferred_element_type=wide
    ).astype(jnp.bfloat16)
    key_grad = jnp.einsum("rkgj,rkgd->jkd", score_grad, query_part, preferred_element_type=wide)
    value_grad = jnp.einsum("rkgj,rkgd->jkd", probs_low, cot_part, preferred_element_type=wide)
    return (context, query_grad, key_grad, value_grad)


def run_keys(query_blocks, cot_blocks, key_rows, value_rows, visible):

    def block_step(totals, slices):
        context, query_grad, key_grad, value_grad = attend_block(
            slices[0], slices[1], key_rows, value_rows, slices[2]
        )
        return ((totals[0] + key_grad, totals[1] + value_grad), (context, query_grad))

    empty_grads = jnp.zeros(key_rows.shape, jnp.float32)
    (key_grad, value_grad), (context, query_grad) = lax.scan(
        block_step, (empty_grads, empty_grads), (query_blocks, cot_blocks, visible)
    )
    return (context, query_grad, key_grad, value_grad)


def local(queries, cotangent, vision, kv_weight, visible_tiles, image_count):
    text_len = queries.shape[1]
    kv_dev = kv_weight.shape[2]
    group_size = HEADS // KV
    block_count = text_len // ROW_BLOCK
    rows_dev = vision.shape[0]
    full_width = vision.shape[1]
    kv_width = kv_dev * 2 * HD
    weights = lax.all_gather(kv_weight, "dp", axis=1, tiled=True)[0]
    image_rows = lax.all_gather(vision, ("section", "tensor"), axis=0, tiled=True)
    key_value = jnp.dot(
        image_rows, weights.reshape(weights.shape[0], kv_width), preferred_element_type=jnp.float32
    )
    key_count = key_value.shape[0]
    key_value = key_value.astype(jnp.bfloat16).reshape(key_count, kv_dev, 2 * HD)
    key_rows = key_value[:, :, :HD]
    value_rows = key_value[:, :, HD:]
    visible = build_visible(visible_tiles[0], image_count[0]).reshape(
        block_count, ROW_BLOCK, key_count
    )
    query_blocks = queries[0].reshape(block_count, ROW_BLOCK, kv_dev, group_size, HD)
    cot_blocks = cotangent[0].reshape(block_count, ROW_BLOCK, kv_dev, group_size, HD)
    context, query_grad, key_grad, value_grad = run_keys(
        query_blocks, cot_blocks, key_rows, value_rows, visible
    )
    context = context.reshape(1, text_len, kv_dev * group_size * HD)
    grad_queries = query_grad.reshape(1, text_len, kv_dev * group_size * HD)
    kv_grad = jnp.concatenate([key_grad, value_grad], axis=-1).astype(jnp.bfloat16)
    weight_term = jnp.einsum(
        "vd,vkc->dkc", image_rows, kv_grad, preferred_element_type=jnp.float32
    )[None]
    grad_kv_weight = lax.psum_scatter(weight_term, "dp", scatter_dimension=1, tiled=True)
    grads_docs = kv_grad[None]
    vision_terms = lax.psum_scatter(
        jnp.einsum("gvkc,dkc->vgd", grads_docs, weights, preferred_element_type=jnp.float32),
        ("section", "tensor"),
        scatter_dimension=0,
        tiled=True,
    )
    grad_vision = vision_terms.reshape(rows_dev, full_width)
    return (context, grad_queries, grad_vision, grad_kv_weight)


def solution(mesh):
    return jax.shard_map(
        local,
        mesh=mesh,
        in_specs=(
            P("section", "dp", "tensor"),
            P("section", "dp", "tensor"),
            P(("dp", "section", "tensor"), None),
            P("section", "dp", "tensor", None),
            P("dp", None, None),
            P("dp"),
        ),
        out_specs=(
            P("section", "dp", "tensor"),
            P("section", "dp", "tensor"),
            P(("dp", "section", "tensor"), None),
            P("section", "dp", "tensor", None),
        ),
        check_vma=False,
    )
```

profile of v0, /device:TPU:0, one launch (start us, length us, event | category | flops | bytes accessed | tf_op | source)
XLA Modules:
  0.0 655.0 jit_solution(656769600232093284)
XLA Ops:
  8.7 5.3 copy.47
  15.0 5.2 copy.48
  21.1 29.8 %all-gather.5.cloned.1.call-done = bf16[1,8192,1,256]{3,1,2,0:T(8,128)(2,1)} async-done(((bf16[1,2048,1,256]{3,1,2,0:T(8,128)(2,1)}), bf16[1,8192,1,256]{3,1,2,0:T(8,128)(2,1)}) %all-gather.5.cloned.1.call-update) | async-done | bytes 4194320 | tf_op jit(solution)/shard_map/all_gather | solution.py:75
  50.8 168.0 %all-gather.3.cloned.1.call-done = bf16[512,8192]{1,0:T(8,128)(2,1)} async-done(((bf16[16,8192]{1,0:T(8,128)(2,1)}), bf16[512,8192]{1,0:T(8,128)(2,1)}) %all-gather.3.cloned.1.call-update) | async-done | bytes 8388624 | tf_op jit(solution)/shard_map/all_gather | solution.py:76
  218.8 6.9 %fusion.43 = bf16[512,1,256]{2,0,1:T(8,128)(2,1)S(1)} fusion(bf16[512,8192]{1,0:T(8,128)(2,1)} %all-gather.3.cloned.1.call-done, bf16[1,8192,1,256]{3,1,2,0:T(8,128)(2,1)} %all-gather.5.cloned.1.call-done), kind=kOutput, calls=%fused_computation.49 | convolution fusion | flops 2147614720 | bytes 12845056 | tf_op jit(solution)/shard_map/dot_general | solution.py:77
  225.8 128.4 %while.17 = (s32[]{:T(128)}, f32[512,1,128]{0,2,1:T(8,128)S(1)}, f32[512,1,128]{0,2,1:T(8,128)S(1)}, bf16[4,512,1,8,128]{4,3,1,0,2:T(8,128)(2,1)}, bf16[4,512,1,...) while((s32[]{:T(128)}, f32[512,1,128]{0,2,1:T(8,128)S(1)}, ...), condition=%wide.region_5.6_spmd.clone, body=%wide.region_0.5_spmd.clone.sunk | while | flops 3287805440 | bytes 182732624 | solution.py:61
  228.2 1.8 fusion.80
  230.1 1.7 fusion.81
  231.8 2.1 constant_dynamic-slice_fusion.7
  233.9 3.3 fusion.82
  237.3 4.3 fusion.83
  241.6 3.9 fusion.84
  245.5 5.2 fusion.85
  252.1 3.3 fusion.87
  255.4 2.7 copy_dynamic-update-slice_fusion.3
  260.3 1.8 fusion.80
  262.1 1.7 fusion.81
  263.9 2.1 constant_dynamic-slice_fusion.7
  266.0 3.3 fusion.82
  269.3 4.3 fusion.83
  273.7 3.9 fusion.84
  277.6 5.2 fusion.85
  284.1 3.3 fusion.87
  287.4 2.7 copy_dynamic-update-slice_fusion.3
  292.4 1.8 fusion.80
  295.9 2.1 constant_dynamic-slice_fusion.7
  298.0 3.3 fusion.82
  301.4 4.3 fusion.83
  305.7 3.9 fusion.84
  309.6 5.2 fusion.85
  316.2 3.3 fusion.87
  319.5 2.7 copy_dynamic-update-slice_fusion.3
  324.4 1.8 fusion.80
  326.2 1.7 fusion.81
  328.0 2.1 constant_dynamic-slice_fusion.7
  330.1 3.3 fusion.82
  333.4 4.3 fusion.83
  337.8 3.9 fusion.84
  341.7 5.2 fusion.85
  348.2 3.3 fusion.87
  351.5 2.7 copy_dynamic-update-slice_fusion.3
  354.2 9.0 %convolution_bitcast_fusion.2 = f32[1,8192,1,256]{1,3,2,0:T(8,128)} fusion(bf16[512,8192]{1,0:T(8,128)(2,1)} %all-gather.3.cloned.1.call-done, bf16[512,128]{0,1:T(8,128)(2,1)S(1)} %get-tuple-element.144, bf16[512,128]{0,1:T(8,128)(2,1)S(1)} %get-tuple-element.145), kind=kOutput, calls=%fused_computation.43 | convolution fusion | flops 2148007936 | bytes 17039360 | tf_op jit(solution)/shard_map/vd,vkc->dkc/dot_general | solution.py:95
  363.3 11.2 %convolution_bitcast_fusion.1 = f32[512,1,8192]{2,0,1:T(8,128)} fusion(bf16[1,8192,1,256]{3,1,2,0:T(8,128)(2,1)} %all-gather.5.cloned.1.call-done, bf16[512,128]{0,1:T(8,128)(2,1)S(1)} %get-tuple-element.144, bf16[512,128]{0,1:T(8,128)(2,1)S(1)} %get-tuple-element.145), kind=kOutput, calls=%fused_computation.42 | convolution fusion | flops 2148007936 | bytes 21233664 | tf_op jit(solution)/shard_map/gvkc,dkc->vgd/dot_general | solution.py:101
  374.5 7.8 %reshape.169 = bf16[1,2048,1024]{2,1,0:T(8,128)(2,1)} reshape(bf16[4,512,1,8,128]{4,3,1,0,2:T(8,128)(2,1)} %get-tuple-element.59) | data formatting | bytes 8388608 | tf_op jit(solution)/shard_map/reshape | solution.py:92
  382.3 7.3 %reshape.170 = bf16[1,2048,1024]{2,1,0:T(8,128)(2,1)} reshape(bf16[4,512,1,8,128]{4,3,1,0,2:T(8,128)(2,1)} %get-tuple-element.60) | data formatting | bytes 8388608 | tf_op jit(solution)/shard_map/reshape | solution.py:93
  389.6 53.4 %reduce-scatter.5.cloned.1.call-done = f32[1,2048,1,256]{1,3,2,0:T(8,128)} async-done(((f32[1,8192,1,256]{1,3,2,0:T(8,128)}), f32[1,2048,1,256]{1,3,2,0:T(8,128)}) %reduce-scatter.5.cloned.1.call-update) | async-done | bytes 2097168 | tf_op jit(solution)/shard_map/reduce_scatter | solution.py:98
  443.0 6.0 copy.32
  449.0 199.4 %reduce-scatter.3.cloned.1.call-done = f32[16,1,8192]{2,0,1:T(8,128)} async-done(((f32[512,1,8192]{2,0,1:T(8,128)}), f32[16,1,8192]{2,0,1:T(8,128)}) %reduce-scatter.3.cloned.1.call-update) | async-done | bytes 524304 | tf_op jit(solution)/shard_map/reduce_scatter | solution.py:100
  (100 shorter events, 18.9 us)
Async XLA Ops:
  7.2 7.5 %copy-start.4 = (s32[1,16,8]{1,2,0:T(8,128)S(1)}, s32[1,16,8]{1,2,0:T(8,128)}, u32[]{:S(2)}) copy-start(s32[1,16,8]{1,2,0:T(8,128)} %param.12) | copy-start | bytes 1540
  7.2 43.7 %all-gather.5.cloned.1.call-start = ((), (), s32[]{:S(2)}) async-start(), calls=%async_computation.3 | async-start | bytes 5242880 | tf_op jit(solution)/shard_map/all_gather | solution.py:75
  7.9 210.9 %all-gather.3.cloned.1.call-start = ((), (), s32[]{:S(2)}) async-start(), calls=%async_computation.2 | async-start | bytes 8650752 | tf_op jit(solution)/shard_map/all_gather | solution.py:76
  8.7 434.3 %reduce-scatter.5.cloned.1.call-start = ((), (), s32[]{:S(2)}) async-start(), calls=%async_computation.5 | async-start | bytes 10485760 | tf_op jit(solution)/shard_map/reduce_scatter | solution.py:98
  226.0 1.0 copy-start.2
  230.1 7.2 %copy-start = (f32[512,8,512]{0,2,1:T(8,128)}, f32[512,8,512]{0,2,1:T(8,128)S(1)}, u32[]{:S(2)}) copy-start(f32[512,8,512]{0,2,1:T(8,128)S(1)} %get-tuple-element.216) | copy-start | bytes 25165828 | tf_op jit(solution)/shard_map/while
  241.6 10.4 %slice-start = ((s8[8388608]{0:T(1024)(128)(4,1)}), s8[4194304]{0:T(1024)(128)(4,1)S(1)}, s32[]{:S(2)}) async-start(s8[8388608]{0:T(1024)(128)(4,1)} %bitcast.227), calls=%async_computation.6 | async-start | bytes 8388608 | tf_op jit(solution)/shard_map/while
  245.5 5.2 copy-start.1
  245.5 6.5 slice-start.1
  252.1 6.0 copy-start.3
  258.0 1.0 copy-start.2
  262.1 7.2 %copy-start = (f32[512,8,512]{0,2,1:T(8,128)}, f32[512,8,512]{0,2,1:T(8,128)S(1)}, u32[]{:S(2)}) copy-start(f32[512,8,512]{0,2,1:T(8,128)S(1)} %get-tuple-element.216) | copy-start | bytes 25165828 | tf_op jit(solution)/shard_map/while
  273.7 10.4 %slice-start = ((s8[8388608]{0:T(1024)(128)(4,1)}), s8[4194304]{0:T(1024)(128)(4,1)S(1)}, s32[]{:S(2)}) async-start(s8[8388608]{0:T(1024)(128)(4,1)} %bitcast.227), calls=%async_computation.6 | async-start | bytes 8388608 | tf_op jit(solution)/shard_map/while
  277.6 5.2 copy-start.1
  277.6 6.5 slice-start.1
  284.1 6.0 copy-start.3
  290.1 1.0 copy-start.2
  294.2 7.2 %copy-start = (f32[512,8,512]{0,2,1:T(8,128)}, f32[512,8,512]{0,2,1:T(8,128)S(1)}, u32[]{:S(2)}) copy-start(f32[512,8,512]{0,2,1:T(8,128)S(1)} %get-tuple-element.216) | copy-start | bytes 25165828 | tf_op jit(solution)/shard_map/while
  305.7 10.4 %slice-start = ((s8[8388608]{0:T(1024)(128)(4,1)}), s8[4194304]{0:T(1024)(128)(4,1)S(1)}, s32[]{:S(2)}) async-start(s8[8388608]{0:T(1024)(128)(4,1)} %bitcast.227), calls=%async_computation.6 | async-start | bytes 8388608 | tf_op jit(solution)/shard_map/while
  309.6 5.2 copy-start.1
  309.6 6.5 slice-start.1
  316.2 6.0 copy-start.3
  322.1 1.0 copy-start.2
  326.2 7.2 %copy-start = (f32[512,8,512]{0,2,1:T(8,128)}, f32[512,8,512]{0,2,1:T(8,128)S(1)}, u32[]{:S(2)}) copy-start(f32[512,8,512]{0,2,1:T(8,128)S(1)} %get-tuple-element.216) | copy-start | bytes 25165828 | tf_op jit(solution)/shard_map/while
  337.8 10.4 %slice-start = ((s8[8388608]{0:T(1024)(128)(4,1)}), s8[4194304]{0:T(1024)(128)(4,1)S(1)}, s32[]{:S(2)}) async-start(s8[8388608]{0:T(1024)(128)(4,1)} %bitcast.227), calls=%async_computation.6 | async-start | bytes 8388608 | tf_op jit(solution)/shard_map/while
  341.7 5.2 copy-start.1
  341.7 6.5 slice-start.1
  348.2 6.0 copy-start.3
  363.2 285.2 %reduce-scatter.3.cloned.1.call-start = ((), (), s32[]{:S(2)}) async-start(), calls=%async_computation.4 | async-start | bytes 17301504 | tf_op jit(solution)/shard_map/reduce_scatter | solution.py:100
Sparse Core Ops, SparseCore 0:
  9.7 41.1 all-gather.4
  52.5 166.3 all-gather.2
  363.3 79.6 reduce-scatter.4
  446.0 202.4 reduce-scatter.2
where the time goes:
time: 656 us; the launch traced here: 655 us
  waiting for transfers between devices  452 us (69%)
  matrix products  102 us (16%)
  local copies, waits for them, and re-layouts  59.7 us (9%)
  other arithmetic  25.7 us (4%)
  between operations  14.5 us (2%)
    reduce_scatter x1, waiting for transfers between devices, local(): lax.psum_scatter(jnp.einsum('gvkc,dkc->vgd', grads_docs, weights, preferr...  199 us
    all_gather x1, waiting for transfers between devices, local(): lax.all_gather(vision, ('section', 'tensor'), axis=0, tiled=True)  168 us
    reduce_scatter x1, waiting for transfers between devices, local(): lax.psum_scatter(weight_term, 'dp', scatter_dimension=1, tiled=True)  53.4 us
    all_gather x1, waiting for transfers between devices, local(): weights = lax.all_gather(kv_weight, 'dp', axis=1, tiled=True)[0]  29.8 us
    dot_general x4, matrix products, attend_block(): jnp.einsum('rkgj,rkgd->jkd', probs_low, cot_part, preferred_element_type=...  20.7 us
    another operation x6, other arithmetic  17.4 us
    unnamed x5, local copies, waits for them, and re-layouts  16.6 us
    dot_general x4, matrix products, attend_block(): jnp.einsum('rkgj,rkgd->jkd', score_grad, query_part, preferred_element_ty...  15.6 us
  transfers between devices with their start and end apart: 4, of which 4 were waited for; matrix products, arithmetic and copies ran while one was open for 7% of the time, Pallas kernels for 0%

commit v1 on v0

v1 whole, which is shorter than its diff:
```python
import jax, jax.numpy as jnp
from jax import lax
from jax.experimental import pallas as pl
from jax.experimental.pallas import tpu as pltpu
from jax.sharding import Mesh
from jax.sharding import PartitionSpec as P

HD=128; GROUP=8; TILES=4; TEXT_BLOCK=128; SEC=8
HIDDEN=-1e30
LOG2E=1.4426950408889634

def attend_kernel(tiles_ref, count_ref, q_ref, cot_ref, kv_ref, ctx_ref, dq_ref, dkv_ref, key_t, value_t, dkey, dvalue):
    block = pl.program_id(0)
    scale = HD ** (-0.5)
    wide = jnp.float32
    low = jnp.bfloat16

    @pl.when(block == 0)
    def _():
        key_t[...] = kv_ref[:, :HD].astype(wide).T.astype(low)
        value_t[...] = kv_ref[:, HD:].astype(wide).T.astype(low)
        dkey[...] = jnp.zeros_like(dkey)
        dvalue[...] = jnp.zeros_like(dvalue)

    seen = [(tiles_ref[block, t] == 1) & (t // TILES < count_ref[0]) for t in range(SEC)]
    any_seen = seen[0]
    for t in range(1, SEC):
        any_seen = any_seen | seen[t]

    @pl.when(jnp.logical_not(any_seen))
    def _():
        ctx_ref[...] = jnp.zeros_like(ctx_ref)
        dq_ref[...] = jnp.zeros_like(dq_ref)

    @pl.when(any_seen)
    def _():
        bias = [jnp.where(s, 0.0, HIDDEN).astype(wide) for s in seen]
        rows = kv_ref.shape[0]
        for pair in range(GROUP // 2):
            at = pair * 2 * HD
            q2 = jnp.concatenate([q_ref[:, at:at + HD], q_ref[:, at + HD:at + 2 * HD]], axis=0)
            g2 = jnp.concatenate([cot_ref[:, at:at + HD], cot_ref[:, at + HD:at + 2 * HD]], axis=0)
            scores = lax.dot_general(kv_ref[:, :HD], q2, (((1,), (1,)), ((), ())), preferred_element_type=wide)
            scores = jnp.concatenate([scores[r * 16:r * 16 + 16] + bias[r % SEC] for r in range(rows // 16)], axis=0)
            peak = jnp.max(scores, axis=0, keepdims=True)
            expon = jnp.exp2((scores - peak) * (scale * LOG2E))
            probs = expon * (1.0 / jnp.sum(expon, axis=0, keepdims=True))
            probs_low = probs.astype(low)
            ctx = jnp.dot(value_t[...], probs_low, preferred_element_type=wide).T.astype(low)
            ctx_ref[:, at:at + HD] = ctx[:TEXT_BLOCK]
            ctx_ref[:, at + HD:at + 2 * HD] = ctx[TEXT_BLOCK:]
            prob_grad = lax.dot_general(kv_ref[:, HD:], g2, (((1,), (1,)), ((), ())), preferred_element_type=wide)
            delta = jnp.sum(probs * prob_grad, axis=0, keepdims=True)
            score_grad = (probs * ((prob_grad - delta) * scale)).astype(low)
            dq = jnp.dot(key_t[...], score_grad, preferred_element_type=wide).T.astype(low)
            dq_ref[:, at:at + HD] = dq[:TEXT_BLOCK]
            dq_ref[:, at + HD:at + 2 * HD] = dq[TEXT_BLOCK:]
            dkey[...] += jnp.dot(score_grad, q2, preferred_element_type=wide)
            dvalue[...] += jnp.dot(probs_low, g2, preferred_element_type=wide)

    @pl.when(block == pl.num_programs(0) - 1)
    def _():
        dkv_ref[:, :HD] = dkey[...].astype(low)
        dkv_ref[:, HD:] = dvalue[...].astype(low)


def attend(tiles, count, queries, cot, kv):
    text, width = queries.shape
    blocks = text // TEXT_BLOCK
    vis = kv.shape[0]
    wide = pl.BlockSpec((TEXT_BLOCK, width), lambda b: (b, 0))
    whole = pl.BlockSpec((vis, 2 * HD), lambda b: (0, 0))
    flops = 12 * text * width * vis
    return pl.pallas_call(
        attend_kernel,
        grid=(blocks,),
        in_specs=[pl.BlockSpec(memory_space=pltpu.SMEM), pl.BlockSpec(memory_space=pltpu.SMEM), wide, wide, whole],
        out_specs=[wide, wide, whole],
        out_shape=[jax.ShapeDtypeStruct(queries.shape, jnp.bfloat16), jax.ShapeDtypeStruct(queries.shape, jnp.bfloat16),
                   jax.ShapeDtypeStruct(kv.shape, jnp.bfloat16)],
        scratch_shapes=[pltpu.VMEM((HD, vis), jnp.bfloat16), pltpu.VMEM((HD, vis), jnp.bfloat16),
                        pltpu.VMEM((vis, HD), jnp.float32), pltpu.VMEM((vis, HD), jnp.float32)],
        compiler_params=pltpu.CompilerParams(vmem_limit_bytes=48 * 1024 * 1024),
        cost_estimate=pl.CostEstimate(flops=flops, bytes_accessed=4 * text * width * 2, transcendentals=text * width // HD * vis),
    )(tiles, count, queries, cot, kv)


DP = ("zh", "co")
SECTION = ("zl", "x")
KV_COLS = 2 * HD


def shift(array, axis, size, step):
    return lax.ppermute(array, axis, [(i, (i + step) % size) for i in range(size)])


def ring_y(array):
    below = shift(array, "y", 4, 1)
    above = shift(array, "y", 4, -1)
    half = array.shape[0] // 2
    first = shift(below[:half], "y", 4, 1)
    second = shift(above[half:], "y", 4, -1)
    return [array, below, above, jnp.concatenate([first, second], axis=0)]


RING = (0, -1, 1, 2)


def local(queries, cotangent, vision, kv_weight, visible_tiles, image_count):
    wide, low = jnp.float32, jnp.bfloat16
    rows, width = vision.shape
    depth = width // 4
    sections = 8
    y = lax.axis_index("y")
    zh = lax.axis_index("zh")
    co = lax.axis_index("co")

    weight = kv_weight.reshape(depth, KV_COLS)
    weights = ring_y(weight)

    own = vision.reshape(rows, 4, depth).transpose(1, 0, 2)
    own = lax.all_to_all(own, DP, 0, 0, tiled=True)
    features = lax.all_to_all(
        jnp.broadcast_to(own[None], (sections,) + own.shape), SECTION, 0, 0, tiled=True
    ).reshape(sections * 4 * rows, depth)

    parts = [jnp.dot(features, w, preferred_element_type=wide).reshape(sections, 4, rows, KV_COLS) for w in weights]
    part = jnp.stack(parts).reshape(4, sections, 2, 2, rows, KV_COLS)
    keep = lax.dynamic_index_in_dim(part, co, 3, keepdims=False)
    away = lax.dynamic_index_in_dim(part, 1 - co, 3, keepdims=False)
    part = keep + shift(away, "co", 2, 1)
    keep = lax.dynamic_index_in_dim(part, zh, 2, keepdims=False)
    away = lax.dynamic_index_in_dim(part, 1 - zh, 2, keepdims=False)
    key_value = (keep + shift(away, "zh", 2, 1)).astype(low)
    pieces = [key_value[j] if step == 0 else shift(key_value[j], "y", 4, step) for j, step in enumerate(RING)]
    kv = jnp.stack(pieces).reshape(4 * sections * rows, KV_COLS)

    features, kv = lax.optimization_barrier((features, kv))
    feature_ring = ring_y(features)

    context, grad_queries, kv_grad = attend(visible_tiles[0], image_count, queries[0], cotangent[0], kv)

    kv_grad = kv_grad.reshape(4, sections, rows, KV_COLS)
    back = [kv_grad[j] if step == 0 else shift(kv_grad[j], "y", 4, -step) for j, step in enumerate(RING)]
    heads = jnp.stack(back)

    def over_dp(block):
        other = shift(block, "zh", 2, 1)
        low_block = jnp.where(zh == 0, block, other)
        high_block = jnp.where(zh == 0, other, block)
        pair = jnp.stack([low_block, high_block])
        pair_other = shift(pair, "co", 2, 1)
        low_pair = jnp.where(co == 0, pair, pair_other)
        high_pair = jnp.where(co == 0, pair_other, pair)
        return jnp.stack([low_pair, high_pair], axis=1)

    all_heads = over_dp(heads).reshape(4, 4, sections, rows, KV_COLS)
    all_heads = all_heads.transpose(1, 2, 0, 3, 4).reshape(4, sections * 4 * rows, KV_COLS)
    vision_part = sum(
        lax.dot_general(all_heads[j], weights[j], (((1,), (1,)), ((), ())), preferred_element_type=wide)
        for j in range(4)
    )
    vision_part = vision_part.astype(low).reshape(sections, 4 * rows, depth)
    vision_part = lax.all_to_all(vision_part, SECTION, 0, 0, tiled=True)
    vision_part = jnp.sum(vision_part.astype(wide), axis=0).astype(low).reshape(4, rows, depth)
    vision_part = lax.all_to_all(vision_part, DP, 0, 0, tiled=True)
    grad_vision = vision_part.transpose(1, 0, 2).reshape(rows, width).astype(wide)

    own_head = over_dp(kv_grad).reshape(4, 4, sections, rows, KV_COLS)
    own_head = own_head.transpose(1, 2, 0, 3, 4).reshape(4, sections * 4 * rows, KV_COLS)
    match = (0, 2, 1, 3)
    grad_weight = sum(
        lax.dot_general(feature_ring[match[j]], own_head[j], (((0,), (0,)), ((), ())), preferred_element_type=wide)
        for j in range(4)
    )
    return (
        context[None],
        grad_queries[None],
        grad_vision,
        grad_weight.reshape(1, depth, 1, KV_COLS),
    )


def solution(mesh):
    fine = Mesh(mesh.devices.reshape(2, 2, 2, 4, 4), ("zh", "co", "zl", "x", "y"))
    return jax.shard_map(
        local,
        mesh=fine,
        in_specs=(
            P(SECTION, DP, "y"),
            P(SECTION, DP, "y"),
            P(DP + SECTION + ("y",), None),
            P(SECTION, DP, "y", None),
            P(DP, None, None),
            P(DP),
        ),
        out_specs=(
            P(SECTION, DP, "y"),
            P(SECTION, DP, "y"),
            P(DP + SECTION + ("y",), None),
            P(SECTION, DP, "y", None),
        ),
        check_vma=False,
    )
```

time: 656 us -> 293 us (0.45)
  waiting for transfers between devices: 452 us -> 102 us
  matrix products: 102 us -> 23.8 us
  Pallas kernels: 0 us -> 69.1 us
  starting transfers between devices: 0.16 us -> 40.2 us
  local copies, waits for them, and re-layouts: 59.7 us -> 34 us
  other arithmetic: 25.7 us -> 8.29 us
  between operations: 14.5 us -> 1.67 us
  blocking collectives: 0 us -> 12.6 us
    reduce_scatter x2 -> x0, waiting for transfers between devices: 253 us -> none  [the longest x1 199 us: local(): lax.psum_scatter(jnp.einsum('gvkc,dkc->vgd', grads_docs, weights, preferr...]
    all_gather x2 -> x0, waiting for transfers between devices: 198 us -> none  [the longest x1 168 us: local(): lax.all_gather(vision, ('section', 'tensor'), axis=0, tiled=True)]
    ppermute x0 -> x20, waiting for transfers between devices: none -> 98.2 us  [shift(): lax.ppermute(array, axis, [(i, (i + step) % size) for i in range(size)])]
    dot_general x27 -> x12, matrix products: 102 us -> 23.8 us  [the longest x4 9.24 us: local(): lax.dot_general(feature_ring[match[j]], own_head[j], (((0,), (0,)), ((),...]
    pallas_call x0 -> x1, Pallas kernels: none -> 69.1 us  [attend(): pl.pallas_call(attend_kernel, grid=(blocks,), in_specs=[pl.BlockSpec(memo...]
    ppermute x0 -> x20, starting transfers between devices: none -> 27.3 us  [shift(): lax.ppermute(array, axis, [(i, (i + step) % size) for i in range(size)])]
    dynamic_slice x12 -> x0, local copies, waits for them, and re-layouts: 15.1 us -> none  [run_keys(): lax.scan(block_step, (empty_grads, empty_grads), (query_blocks, cot_block...]
    another operation x6 -> x11, other arithmetic: 17.4 us -> 2.65 us  [the longest x4 1.93 us: over_dp(): pair = jnp.stack([low_block, high_block])]
  transfers between devices with their start and end apart: 4 -> 23, of which waited for: 4 -> 16; matrix products, arithmetic and copies ran while one was open for 7% -> 9% of each run, Pallas kernels for 0% -> 0%
where the time goes in v1:
time: 293 us; the launch traced here: 291 us
  waiting for transfers between devices  102 us (35%)
  Pallas kernels  69.1 us (24%)
  starting transfers between devices  40.2 us (14%)
  local copies, waits for them, and re-layouts  34 us (12%)
  matrix products  23.8 us (8%)
  blocking collectives  12.6 us (4%)
  other arithmetic  8.29 us (3%)
    ppermute x20, waiting for transfers between devices, shift(): lax.ppermute(array, axis, [(i, (i + step) % size) for i in range(size)])  98.2 us
    pallas_call x1, Pallas kernels, attend(): pl.pallas_call(attend_kernel, grid=(blocks,), in_specs=[pl.BlockSpec(memo...  69.1 us
    ppermute x20, starting transfers between devices, shift(): lax.ppermute(array, axis, [(i, (i + step) % size) for i in range(size)])  27.3 us
    unnamed x28, local copies, waits for them, and re-layouts  18.9 us
    all_to_all x1, blocking collectives, local(): own = lax.all_to_all(own, DP, 0, 0, tiled=True)  12.6 us
    dot_general x4, matrix products, local(): lax.dot_general(feature_ring[match[j]], own_head[j], (((0,), (0,)), ((),...  9.24 us
    dot_general x4, matrix products, local(): jnp.dot(features, w, preferred_element_type=wide)  8.9 us
  transfers between devices with their start and end apart: 23, of which 16 were waited for; matrix products, arithmetic and copies ran while one was open for 9% of the time, Pallas kernels for 0%

profile of v1, /device:TPU:0, one launch (start us, length us, event | category | flops | bytes accessed | tf_op | source)
XLA Modules:
  0.0 291.4 jit_solution(18198249927959572719)
XLA Ops:
  1.6 12.6 %all_to_all.20 = bf16[4,16,2048]{2,1,0:T(8,128)(2,1)S(1)} all-to-all(bf16[4,16,2048]{2,1,0:T(8,128)(2,1)S(1)} %bitcast.144), channel_id=1, replica_groups=mesh['zh'=2,'co'=2,'zl'=2,'x'=4,'y'=4] {'zh','co'}, dimensions={0} | all-to-all | bytes 524288 | tf_op jit(solution)/shard_map/all_to_all | solution.py:122
  14.2 1.6 broadcast_in_dim.12
  15.7 4.8 %all-to-all-start.1 = ((bf16[8,4,16,2048]{3,2,1,0:T(8,128)(2,1)}), bf16[8,4,16,2048]{3,2,1,0:T(8,128)(2,1)S(1)}, u32[]{:S(2)}, u32[]{:S(2)}) async-start(bf16[8,4,16,2048]{3,2,1,0:T(8,128)(2,1)} %broadcast_in_dim.12), calls=%async_computation.1 | async-start | bytes 4194304 | tf_op jit(solution)/shard_map/all_to_all | solution.py:123
  20.5 1.6 collective-permute-start
  22.1 1.7 collective-permute-start.1
  23.7 22.5 %collective-permute-done = bf16[2048,256]{1,0:T(8,128)(2,1)S(1)} collective-permute-done((bf16[2048,256]{1,0:T(8,128)(2,1)}, bf16[2048,256]{1,0:T(8,128)(2,1)S(1)}, u32[]{:S(2)}, u32[]{:S(2)}) %collective-permute-start) | collective-permute-done | bytes 1048608 | tf_op jit(solution)/shard_map/ppermute | solution.py:94
  49.3 2.9 %collective-permute-start.3 = (bf16[1024,256]{1,0:T(8,128)(2,1)}, bf16[1024,256]{1,0:T(8,128)(2,1)}, u32[]{:S(2)}, u32[]{:S(2)}) collective-permute-start(bf16[1024,256]{1,0:T(8,128)(2,1)} %slice.96), channel_id=1, source_target_pairs={{0,3},{1,0},{2,1},{3,2},{4,7},{5,4},{6,5},{7,6},{8,11},{9,8},{10,9... | collective-permute-start | bytes 1572872 | tf_op jit(solution)/shard_map/ppermute | solution.py:94
  52.3 8.6 %collective-permute-done.2 = bf16[1024,256]{1,0:T(8,128)(2,1)} collective-permute-done((bf16[1024,256]{1,0:T(8,128)(2,1)}, bf16[1024,256]{1,0:T(8,128)(2,1)}, u32[]{:S(2)}, u32[]{:S(2)}) %collective-permute-start.2) | collective-permute-done | bytes 524320 | tf_op jit(solution)/shard_map/ppermute | solution.py:94
  60.8 1.9 constant_dynamic-update-slice_fusion.1
  62.7 1.9 constant_dynamic-update-slice_fusion
  64.6 3.5 %convolution_bitcast_fusion.1 = f32[1,8,2,2,16,256]{5,4,3,2,1,0:T(8,128)} fusion(bf16[8,2,2,16,2048]{4,3,2,1,0:T(8,128)(2,1)S(1)} %bitcast.131, bf16[1,2048,1,256]{3,1,2,0:T(8,128)(2,1)} %param.9), kind=kOutput, calls=%fused_computation.11 | convolution fusion | flops 536870912 | bytes 3670016 | tf_op jit(solution)/shard_map/dot_general | solution.py:127
  68.1 2.8 convolution_bitcast_fusion
  70.9 2.0 copy.29
  72.9 1.9 fusion.6
  76.4 1.3 copy-done.4
  77.9 2.8 collective-permute-done.4
  80.6 1.8 bitcast_add_fusion
  83.3 1.9 collective-permute-start.5
  85.2 13.9 %collective-permute-done.5 = f32[4,8,16,256]{3,2,1,0:T(8,128)} collective-permute-done((f32[4,8,16,256]{3,2,1,0:T(8,128)}, f32[4,8,16,256]{3,2,1,0:T(8,128)}, u32[]{:S(2)}, u32[]{:S(2)}) %collective-permute-start.5) | collective-permute-done | bytes 524320 | tf_op jit(solution)/shard_map/ppermute | solution.py:94
  99.1 1.1 fusion.11
  100.2 1.7 collective-permute-start.8
  101.9 2.2 collective-permute-start.7
  106.1 1.2 collective-permute-done.7
  108.4 2.2 copy-done
  110.6 69.1 %shard_map.93 = (bf16[2048,1024]{1,0:T(8,128)(2,1)}, bf16[2048,1024]{1,0:T(8,128)(2,1)}, bf16[512,256]{1,0:T(8,128)(2,1)S(1)}) custom-call(s32[16,8]{1,0:T(8,128)S(1)} %copy.30.tiles_ref, s32[1]{0:T(128)S(6)} %copy.51.count_ref, bf16[2048,1024]{1,0:T(8,128)(2,1)S(1)} %bitcast.130, bf16[2048,1024]{1,0:T(8,128)(2,1)} %bitcast.170, bf16[512,256]{1,0:T(8,128)(2,1)S(1)} %bitcast.129), custom_call_target="tpu_custom_call" | custom-call | flops 12884901888 | bytes 16777216 | tf_op jit(solution)/shard_map/pallas_call | solution.py:74
  180.4 2.0 collective-permute-start.10
  182.9 2.7 collective-permute-done.11
  185.8 2.1 collective-permute-done.9
  187.9 2.2 collective-permute-start.12
  190.1 6.0 %collective-permute-done.12 = bf16[4,8,16,256]{3,2,1,0:T(8,128)(2,1)S(1)} collective-permute-done((bf16[4,8,16,256]{3,2,1,0:T(8,128)(2,1)S(1)}, bf16[4,8,16,256]{3,2,1,0:T(8,128)(2,1)S(1)}, u32[]{:S(2)}, u32[]{:S(2)}) %collective-permute-start.12) | collective-permute-done | bytes 262176 | tf_op jit(solution)/shard_map/ppermute | solution.py:94
  197.0 3.2 %collective-permute-start.16 = (bf16[512,2048]{1,0:T(8,128)(2,1)S(1)}, bf16[512,2048]{1,0:T(8,128)(2,1)}, u32[]{:S(2)}, u32[]{:S(2)}) collective-permute-start(bf16[512,2048]{1,0:T(8,128)(2,1)S(1)} %bitcast.134), channel_id=1, source_target_pairs={{0,3},{1,0},{2,1},{3,2},{4,7},{5,4},{6,5},{7,6},{8,11},{9,8},{10,9... | collective-permute-start | bytes 6291464 | tf_op jit(solution)/shard_map/ppermute | solution.py:94
  200.2 1.9 collective-permute-start.14
  206.8 3.4 %add_convert_fusion = bf16[512,2048]{1,0:T(8,128)(2,1)} fusion(f32[512,2048]{1,0:T(8,128)S(1)} %fusion.20, f32[512,2048]{1,0:T(8,128)S(1)} %fusion.13, f32[512,2048]{1,0:T(8,128)S(1)} %fusion.19, bf16[512,256]{1,0:T(8,128)(2,1)S(1)} %bitcast.140, bf16[2048,256]{1,0:T(8,128)(2,1)} %constant_dynamic-update-slice_fusion), kind=kOutput, calls=%fused_computation | convolution fusion | flops 541065216 | bytes 15990784 | tf_op jit(solution)/shard_map/dot_general | solution.py:160
  210.2 4.5 %all-to-all-start.2 = ((bf16[8,64,2048]{2,1,0:T(8,128)(2,1)}), bf16[8,64,2048]{2,1,0:T(8,128)(2,1)}, u32[]{:S(2)}, u32[]{:S(2)}) async-start(bf16[8,64,2048]{2,1,0:T(8,128)(2,1)} %bitcast.136), calls=%async_computation.2 | async-start | bytes 4194304 | tf_op jit(solution)/shard_map/all_to_all | solution.py:164
  215.8 1.9 collective-permute-done.15
  218.2 28.1 %collective-permute-done.17 = bf16[512,2048]{1,0:T(8,128)(2,1)} collective-permute-done((bf16[512,2048]{1,0:T(8,128)(2,1)S(1)}, bf16[512,2048]{1,0:T(8,128)(2,1)}, u32[]{:S(2)}, u32[]{:S(2)}) %collective-permute-start.17) | collective-permute-done | bytes 2097184 | tf_op jit(solution)/shard_map/ppermute | solution.py:94
  246.3 2.3 slice.108
  248.7 2.3 slice.109
  251.0 3.2 %collective-permute-start.19 = (bf16[256,2048]{1,0:T(8,128)(2,1)}, bf16[256,2048]{1,0:T(8,128)(2,1)}, u32[]{:S(2)}, u32[]{:S(2)}) collective-permute-start(bf16[256,2048]{1,0:T(8,128)(2,1)} %slice.109), channel_id=1, source_target_pairs={{0,3},{1,0},{2,1},{3,2},{4,7},{5,4},{6,5},{7,6},{8,11},{9,8},{10,9... | collective-permute-start | bytes 3145736 | tf_op jit(solution)/shard_map/ppermute | solution.py:94
  255.0 2.7 reduce_sum.12
  257.7 3.6 %all-to-all-start.3 = ((bf16[4,16,2048]{2,1,0:T(8,128)(2,1)}), bf16[4,16,2048]{2,1,0:T(8,128)(2,1)S(1)}, u32[]{:S(2)}, u32[]{:S(2)}) async-start(bf16[4,16,2048]{2,1,0:T(8,128)(2,1)} %bitcast.51), calls=%async_computation.3 | async-start | bytes 524288 | tf_op jit(solution)/shard_map/all_to_all | solution.py:166
  261.4 3.7 %convolution_add_fusion.1 = f32[2048,256]{1,0:T(8,128)} fusion(f32[2048,256]{1,0:T(8,128)S(1)} %fusion.21, bf16[512,2048]{1,0:T(8,128)(2,1)} %collective-permute-done.16, bf16[512,256]{1,0:T(8,128)(2,1)S(1)} %bitcast.143), kind=kOutput, calls=%fused_computation.4 | convolution fusion | flops 537395200 | bytes 6553600 | tf_op jit(solution)/shard_map/dot_general | solution.py:173
  265.0 3.6 %all-to-all-done.3 = bf16[4,16,2048]{2,1,0:T(8,128)(2,1)S(1)} async-done(((bf16[4,16,2048]{2,1,0:T(8,128)(2,1)}), bf16[4,16,2048]{2,1,0:T(8,128)(2,1)S(1)}, u32[]{:S(2)}, u32[]{:S(2)}) %all-to-all-start.3) | async-done | bytes 262176 | tf_op jit(solution)/shard_map/all_to_all | solution.py:166
  269.5 5.4 %collective-permute-done.18 = bf16[256,2048]{1,0:T(8,128)(2,1)} collective-permute-done((bf16[256,2048]{1,0:T(8,128)(2,1)}, bf16[256,2048]{1,0:T(8,128)(2,1)}, u32[]{:S(2)}, u32[]{:S(2)}) %collective-permute-start.18) | collective-permute-done | bytes 1048608 | tf_op jit(solution)/shard_map/ppermute | solution.py:94
  275.0 1.6 collective-permute-done.19
  276.6 2.4 fusion.2
  279.0 2.4 fusion.1
  281.5 10.0 %copy.42 = f32[1,2048,1,256]{3,2,1,0:T(1,128)} copy(f32[1,2048,1,256]{3,1,2,0:T(8,128)S(1)} %fusion.1) | data formatting | bytes 4194304
  (80 shorter events, 19.1 us)
Async XLA Ops:
  15.7 48.9 %all-to-all-start.1 = ((bf16[8,4,16,2048]{3,2,1,0:T(8,128)(2,1)}), bf16[8,4,16,2048]{3,2,1,0:T(8,128)(2,1)S(1)}, u32[]{:S(2)}, u32[]{:S(2)}) async-start(bf16[8,4,16,2048]{3,2,1,0:T(8,128)(2,1)} %broadcast_in_dim.12), calls=%async_computation.1 | async-start | bytes 4194304 | tf_op jit(solution)/shard_map/all_to_all | solution.py:123
  20.5 25.7 %collective-permute-start = (bf16[2048,256]{1,0:T(8,128)(2,1)}, bf16[2048,256]{1,0:T(8,128)(2,1)S(1)}, u32[]{:S(2)}, u32[]{:S(2)}) collective-permute-start(bf16[2048,256]{1,0:T(8,128)(2,1)} %bitcast.145), channel_id=1, source_target_pairs={{0,1},{1,2},{2,3},{3,0},{4,5},{5,6},{6,7},{7,4},{8,9},{9,10},{10,1... | collective-permute-start | bytes 3145736 | tf_op jit(solution)/shard_map/ppermute | solution.py:94
  22.1 25.4 %collective-permute-start.1 = (bf16[2048,256]{1,0:T(8,128)(2,1)}, bf16[2048,256]{1,0:T(8,128)(2,1)S(1)}, u32[]{:S(2)}, u32[]{:S(2)}) collective-permute-start(bf16[2048,256]{1,0:T(8,128)(2,1)} %bitcast.146), channel_id=1, source_target_pairs={{0,3},{1,0},{2,1},{3,2},{4,7},{5,4},{6,5},{7,6},{8,11},{9,8},{10,9... | collective-permute-start | bytes 3145736 | tf_op jit(solution)/shard_map/ppermute | solution.py:94
  46.2 28.6 %copy-start.5 = (bf16[2048,256]{1,0:T(8,128)(2,1)}, bf16[2048,256]{1,0:T(8,128)(2,1)S(1)}, u32[]{:S(2)}) copy-start(bf16[2048,256]{1,0:T(8,128)(2,1)S(1)} %collective-permute-done) | copy-start | bytes 3145732
  47.1 13.7 %collective-permute-start.2 = (bf16[1024,256]{1,0:T(8,128)(2,1)}, bf16[1024,256]{1,0:T(8,128)(2,1)}, u32[]{:S(2)}, u32[]{:S(2)}) collective-permute-start(bf16[1024,256]{1,0:T(8,128)(2,1)} %slice.95), channel_id=1, source_target_pairs={{0,1},{1,2},{2,3},{3,0},{4,5},{5,6},{6,7},{7,4},{8,9},{9,10},{10,1... | collective-permute-start | bytes 1572872 | tf_op jit(solution)/shard_map/ppermute | solution.py:94
  47.4 1.1 copy-start.7
  49.3 13.4 %collective-permute-start.3 = (bf16[1024,256]{1,0:T(8,128)(2,1)}, bf16[1024,256]{1,0:T(8,128)(2,1)}, u32[]{:S(2)}, u32[]{:S(2)}) collective-permute-start(bf16[1024,256]{1,0:T(8,128)(2,1)} %slice.96), channel_id=1, source_target_pairs={{0,3},{1,0},{2,1},{3,2},{4,7},{5,4},{6,5},{7,6},{8,11},{9,8},{10,9... | collective-permute-start | bytes 1572872 | tf_op jit(solution)/shard_map/ppermute | solution.py:94
  64.6 132.4 %copy-start.2 = (bf16[8,4,16,2048]{3,2,1,0:T(8,128)(2,1)}, bf16[8,4,16,2048]{3,2,1,0:T(8,128)(2,1)S(1)}, u32[]{:S(2)}) copy-start(bf16[8,4,16,2048]{3,2,1,0:T(8,128)(2,1)S(1)} %all-to-all-done.1) | copy-start | bytes 6291460
  74.9 1.0 copy-start.9
  74.9 1.2 copy-start.11
  76.4 1.3 copy-start.4
  77.8 2.9 collective-permute-start.4
  82.4 23.4 %copy-start.12 = (s32[1,16,8]{1,2,0:T(8,128)S(1)}, s32[1,16,8]{1,2,0:T(8,128)}, u32[]{:S(2)}) copy-start(s32[1,16,8]{1,2,0:T(8,128)} %param.10) | copy-start | bytes 1540
  83.3 15.8 %collective-permute-start.5 = (f32[4,8,16,256]{3,2,1,0:T(8,128)}, f32[4,8,16,256]{3,2,1,0:T(8,128)}, u32[]{:S(2)}, u32[]{:S(2)}) collective-permute-start(f32[4,8,16,256]{3,2,1,0:T(8,128)} %dynamic-slice_bitcast_fusion.1), channel_id=1, source_target_pairs={{0,64},{64,0},{1,65},{65,1},{2,66},{66,2},{3,67},{67,3},{4,68},{68... | collective-permute-start | bytes 1572872 | tf_op jit(solution)/shard_map/ppermute | solution.py:94
  100.2 5.9 %collective-permute-start.8 = (bf16[8,16,256]{2,1,0:T(8,128)(2,1)S(1)}, bf16[8,16,256]{2,1,0:T(8,128)(2,1)S(1)}, u32[]{:S(2)}, u32[]{:S(2)}) collective-permute-start(bf16[8,16,256]{2,1,0:T(8,128)(2,1)S(1)} %get-tuple-element.47), channel_id=1, source_target_pairs={{0,2},{1,3},{2,0},{3,1},{4,6},{5,7},{6,4},{7,5},{8,10},{9,11},{10,... | collective-permute-start | bytes 196616 | tf_op jit(solution)/shard_map/ppermute | solution.py:94
  101.9 5.5 %collective-permute-start.7 = (bf16[8,16,256]{2,1,0:T(8,128)(2,1)S(1)}, bf16[8,16,256]{2,1,0:T(8,128)(2,1)S(1)}, u32[]{:S(2)}, u32[]{:S(2)}) collective-permute-start(bf16[8,16,256]{2,1,0:T(8,128)(2,1)S(1)} %get-tuple-element.48), channel_id=1, source_target_pairs={{0,1},{1,2},{2,3},{3,0},{4,5},{5,6},{6,7},{7,4},{8,9},{9,10},{10,1... | collective-permute-start | bytes 196616 | tf_op jit(solution)/shard_map/ppermute | solution.py:94
  104.1 4.3 %collective-permute-start.6 = (bf16[8,16,256]{2,1,0:T(8,128)(2,1)S(1)}, bf16[8,16,256]{2,1,0:T(8,128)(2,1)S(1)}, u32[]{:S(2)}, u32[]{:S(2)}) collective-permute-start(bf16[8,16,256]{2,1,0:T(8,128)(2,1)S(1)} %get-tuple-element.49), channel_id=1, source_target_pairs={{0,3},{1,0},{2,1},{3,2},{4,7},{5,4},{6,5},{7,6},{8,11},{9,8},{10,9... | collective-permute-start | bytes 196616 | tf_op jit(solution)/shard_map/ppermute | solution.py:94
  108.4 2.2 copy-start
  179.7 6.0 %collective-permute-start.11 = (bf16[8,16,256]{2,1,0:T(8,128)(2,1)S(1)}, bf16[8,16,256]{2,1,0:T(8,128)(2,1)S(1)}, u32[]{:S(2)}, u32[]{:S(2)}) collective-permute-start(bf16[8,16,256]{2,1,0:T(8,128)(2,1)S(1)} %bitcast.168), channel_id=1, source_target_pairs={{0,2},{1,3},{2,0},{3,1},{4,6},{5,7},{6,4},{7,5},{8,10},{9,11},{10,... | collective-permute-start | bytes 196616 | tf_op jit(solution)/shard_map/ppermute | solution.py:94
  180.4 5.4 %collective-permute-start.10 = (bf16[8,16,256]{2,1,0:T(8,128)(2,1)S(1)}, bf16[8,16,256]{2,1,0:T(8,128)(2,1)S(1)}, u32[]{:S(2)}, u32[]{:S(2)}) collective-permute-start(bf16[8,16,256]{2,1,0:T(8,128)(2,1)S(1)} %bitcast.167), channel_id=1, source_target_pairs={{0,3},{1,0},{2,1},{3,2},{4,7},{5,4},{6,5},{7,6},{8,11},{9,8},{10,9... | collective-permute-start | bytes 196616 | tf_op jit(solution)/shard_map/ppermute | solution.py:94
  182.4 5.5 %collective-permute-start.9 = (bf16[8,16,256]{2,1,0:T(8,128)(2,1)S(1)}, bf16[8,16,256]{2,1,0:T(8,128)(2,1)S(1)}, u32[]{:S(2)}, u32[]{:S(2)}) collective-permute-start(bf16[8,16,256]{2,1,0:T(8,128)(2,1)S(1)} %bitcast.165), channel_id=1, source_target_pairs={{0,1},{1,2},{2,3},{3,0},{4,5},{5,6},{6,7},{7,4},{8,9},{9,10},{10,1... | collective-permute-start | bytes 196616 | tf_op jit(solution)/shard_map/ppermute | solution.py:94
  187.9 8.1 %collective-permute-start.12 = (bf16[4,8,16,256]{3,2,1,0:T(8,128)(2,1)S(1)}, bf16[4,8,16,256]{3,2,1,0:T(8,128)(2,1)S(1)}, u32[]{:S(2)}, u32[]{:S(2)}) collective-permute-start(bf16[4,8,16,256]{3,2,1,0:T(8,128)(2,1)S(1)} %pad_maximum_fusion.6), channel_id=1, source_target_pairs={{0,64},{64,0},{1,65},{65,1},{2,66},{66,2},{3,67},{67,3},{4,68},{68... | collective-permute-start | bytes 786440 | tf_op jit(solution)/shard_map/ppermute | solution.py:94
  197.0 5.2 %collective-permute-start.13 = (bf16[2,4,8,16,256]{4,3,2,1,0:T(8,128)(2,1)}, bf16[2,4,8,16,256]{4,3,2,1,0:T(8,128)(2,1)S(1)}, u32[]{:S(2)}, u32[]{:S(2)}) collective-permute-start(bf16[2,4,8,16,256]{4,3,2,1,0:T(8,128)(2,1)} %pad_maximum_fusion.3), channel_id=1, source_target_pairs={{0,32},{32,0},{1,33},{33,1},{2,34},{34,2},{3,35},{35,3},{4,36},{36... | collective-permute-start | bytes 1572872 | tf_op jit(solution)/shard_map/ppermute | solution.py:94
  197.0 49.4 %collective-permute-start.17 = (bf16[512,2048]{1,0:T(8,128)(2,1)S(1)}, bf16[512,2048]{1,0:T(8,128)(2,1)}, u32[]{:S(2)}, u32[]{:S(2)}) collective-permute-start(bf16[512,2048]{1,0:T(8,128)(2,1)S(1)} %bitcast.133), channel_id=1, source_target_pairs={{0,1},{1,2},{2,3},{3,0},{4,5},{5,6},{6,7},{7,4},{8,9},{9,10},{10,1... | collective-permute-start | bytes 6291464 | tf_op jit(solution)/shard_map/ppermute | solution.py:94
  197.0 51.7 %collective-permute-start.16 = (bf16[512,2048]{1,0:T(8,128)(2,1)S(1)}, bf16[512,2048]{1,0:T(8,128)(2,1)}, u32[]{:S(2)}, u32[]{:S(2)}) collective-permute-start(bf16[512,2048]{1,0:T(8,128)(2,1)S(1)} %bitcast.134), channel_id=1, source_target_pairs={{0,3},{1,0},{2,1},{3,2},{4,7},{5,4},{6,5},{7,6},{8,11},{9,8},{10,9... | collective-permute-start | bytes 6291464 | tf_op jit(solution)/shard_map/ppermute | solution.py:94
  200.2 14.4 %collective-permute-start.14 = (bf16[4,8,16,256]{3,2,1,0:T(8,128)(2,1)S(1)}, bf16[4,8,16,256]{3,2,1,0:T(8,128)(2,1)}, u32[]{:S(2)}, u32[]{:S(2)}) collective-permute-start(bf16[4,8,16,256]{3,2,1,0:T(8,128)(2,1)S(1)} %bitcast.127), channel_id=1, source_target_pairs={{0,64},{64,0},{1,65},{65,1},{2,66},{66,2},{3,67},{67,3},{4,68},{68... | collective-permute-start | bytes 786440 | tf_op jit(solution)/shard_map/ppermute | solution.py:94
  202.3 1.2 copy-start.10
  203.6 1.2 copy-start.8
  204.8 1.2 copy-start.6
  210.2 44.8 %all-to-all-start.2 = ((bf16[8,64,2048]{2,1,0:T(8,128)(2,1)}), bf16[8,64,2048]{2,1,0:T(8,128)(2,1)}, u32[]{:S(2)}, u32[]{:S(2)}) async-start(bf16[8,64,2048]{2,1,0:T(8,128)(2,1)} %bitcast.136), calls=%async_computation.2 | async-start | bytes 4194304 | tf_op jit(solution)/shard_map/all_to_all | solution.py:164
  215.7 2.0 collective-permute-start.15
  218.2 36.1 %copy-start.3 = (bf16[8,4,16,2048]{3,2,1,0:T(8,128)(2,1)S(1)}, bf16[8,4,16,2048]{3,2,1,0:T(8,128)(2,1)}, u32[]{:S(2)}) copy-start(bf16[8,4,16,2048]{3,2,1,0:T(8,128)(2,1)} %copy-done.2) | copy-start | bytes 6291460
  248.7 26.3 %collective-permute-start.18 = (bf16[256,2048]{1,0:T(8,128)(2,1)}, bf16[256,2048]{1,0:T(8,128)(2,1)}, u32[]{:S(2)}, u32[]{:S(2)}) collective-permute-start(bf16[256,2048]{1,0:T(8,128)(2,1)} %slice.108), channel_id=1, source_target_pairs={{0,1},{1,2},{2,3},{3,0},{4,5},{5,6},{6,7},{7,4},{8,9},{9,10},{10,1... | collective-permute-start | bytes 3145736 | tf_op jit(solution)/shard_map/ppermute | solution.py:94
  251.0 25.6 %collective-permute-start.19 = (bf16[256,2048]{1,0:T(8,128)(2,1)}, bf16[256,2048]{1,0:T(8,128)(2,1)}, u32[]{:S(2)}, u32[]{:S(2)}) collective-permute-start(bf16[256,2048]{1,0:T(8,128)(2,1)} %slice.109), channel_id=1, source_target_pairs={{0,3},{1,0},{2,1},{3,2},{4,7},{5,4},{6,5},{7,6},{8,11},{9,8},{10,9... | collective-permute-start | bytes 3145736 | tf_op jit(solution)/shard_map/ppermute | solution.py:94
  257.7 10.9 %all-to-all-start.3 = ((bf16[4,16,2048]{2,1,0:T(8,128)(2,1)}), bf16[4,16,2048]{2,1,0:T(8,128)(2,1)S(1)}, u32[]{:S(2)}, u32[]{:S(2)}) async-start(bf16[4,16,2048]{2,1,0:T(8,128)(2,1)} %bitcast.51), calls=%async_computation.3 | async-start | bytes 524288 | tf_op jit(solution)/shard_map/all_to_all | solution.py:166
  276.6 2.4 copy-start.1
